TPU v7x, 1024 devices: a whole 8x8x8 slice. The times are simulated.
1024 devices in a mesh: fsdp: 64 (over x, z), dp: 16 (over y, core).
Axes of the slice: x: 8, y: 8, z: 8, core: 2. Of those that a mesh axis runs over, the one named last changes fastest.
Arguments:
- grad_out: bfloat16 [4096, 8192], P('dp', 'fsdp'), may hold values from -6 to 6
- hidden: bfloat16 [4096, 28672], P('dp', 'fsdp'), may hold values from -6 to 6
- base_weight: bfloat16 [28672, 8192], P('fsdp'), may hold values from -0.0625 to 0.0625
- adapt_a: float32 [28672, 16], P('fsdp'), may hold values from -1.5 to 1.5
- adapt_b: float32 [16, 8192], P(None, 'fsdp'), may hold values from -0.0625 to 0.0625
- delta_vals: float32 [1024, 64, 64], P('fsdp'), may hold values from -0.75 to 0.75
- blk_row: int32 [1024], P('fsdp'), may hold values from 0 to 6, as said below
- blk_col: int32 [1024], P('fsdp'), may hold values from 0 to 127
- blk_count: int32 [64], P('fsdp'), may hold values from 1 to 16, as said below
Outputs:
- grad_hidden: bfloat16 [4096, 28672], P('dp', 'fsdp')
- grad_a: float32 [28672, 16], P('fsdp')
- grad_b: float32 [16, 8192], P(None, 'fsdp')
- grad_delta: float32 [1024, 64, 64], P('fsdp')
Inputs may be any that keep to these rules, and one draw needn't show every extreme that they name: `blk_row`: each owner's slots name distinct blocks of its stripe. `blk_count`: some owner has all 16 slots live.
All inputs are finite; a program needn't handle non-finite values.
Results may differ from a plain program's by a relative error of at most 0.0013.
Values may be sent and summed in bfloat16 or wider, within the bound.
A program may use at most 32 MiB of HBM per device.

v0:
```python
import jax
import jax.numpy as jnp
from jax import lax
from jax.sharding import PartitionSpec as P


def pick_columns(source, offsets, width):

    def one_slot(offset):
        return lax.dynamic_slice_in_dim(source, offset, width, 1)

    return jax.vmap(one_slot)(offsets)


def on_device(
    grad_out, hidden, base_weight, adapt_a, adapt_b, delta_vals, blk_row, blk_col, blk_count
):
    highest = lax.Precision.HIGHEST
    tok_rows = grad_out.shape[0]
    local_rows = hidden.shape[1]
    slot_count = blk_row.shape[0]
    block = delta_vals.shape[1]
    stripe = local_rows // block
    flags = (lax.iota(jnp.int32, slot_count) < blk_count[0]).astype(jnp.float32)
    gy_wide = grad_out.astype(jnp.float32)
    h_wide = hidden.astype(jnp.float32)
    part_gb = jnp.dot(gy_wide, adapt_b.T, precision=highest)
    part_ha = jnp.dot(h_wide, adapt_a, precision=highest)
    gy_b, h_a = lax.psum((part_gb, part_ha), "fsdp")
    col_starts = blk_col * block
    gy_full = lax.all_gather(grad_out, "fsdp", axis=1, tiled=True)
    dense = jnp.dot(gy_full, base_weight.T, preferred_element_type=jnp.float32)
    chosen = pick_columns(gy_full, col_starts, block)

    def pick_rows(row_block):
        return lax.dynamic_slice_in_dim(hidden, row_block * block, block, 1)

    row_pieces = jax.vmap(pick_rows)(blk_row)
    grad_blocks = (
        jnp.einsum("ktr,ktc->krc", row_pieces, chosen, preferred_element_type=jnp.float32)
        * flags[:, None, None]
    )
    contrib = (
        jnp.einsum("ktc,krc->ktr", chosen.astype(jnp.float32), delta_vals, precision=highest)
        * flags[:, None, None]
    )
    placing = (blk_row[:, None] == lax.iota(jnp.int32, stripe)[None, :]).astype(jnp.float32)
    sparse = jnp.einsum("kb,ktr->tbr", placing, contrib, precision=highest).reshape(
        tok_rows, local_rows
    )
    grad_hidden = (dense + jnp.dot(gy_b, adapt_a.T, precision=highest) + sparse).astype(
        jnp.bfloat16
    )
    local_ga = jnp.dot(h_wide.T, gy_b, precision=highest)
    local_gb = jnp.dot(h_a.T, gy_wide, precision=highest)
    grad_a, grad_b, grad_delta = lax.psum((local_ga, local_gb, grad_blocks), "dp")
    return (grad_hidden, grad_a, grad_b, grad_delta)


def solution(mesh):
    placed = (
        P("dp", "fsdp"),
        P("dp", "fsdp"),
        P("fsdp", None),
        P("fsdp", None),
        P(None, "fsdp"),
        P("fsdp", None, None),
        P("fsdp"),
        P("fsdp"),
        P("fsdp"),
    )
    return jax.shard_map(
        on_device,
        mesh=mesh,
        in_specs=placed,
        out_specs=(P("dp", "fsdp"), P("fsdp", None), P(None, "fsdp"), P("fsdp", None, None)),
        check_vma=False,
    )
```

profile of v0, /device:TPU:1, one launch (start us, length us, event | category | flops | bytes accessed | tf_op | source)
XLA Modules:
  0.0 550.5 jit_solution(11459631051640071424)
XLA Ops:
  10.9 1.4 fusion.11
  12.4 237.9 %all-reduce.2 = (f32[256,16]{0,1:T(8,128)S(1)}, f32[256,16]{1,0:T(8,128)S(1)}) all-reduce(f32[256,16]{0,1:T(8,128)S(1)} %fusion.9, f32[256,16]{1,0:T(8,128)S(1)} %fusion.11), channel_id=1, replica_groups=mesh['fsdp'=64,'dp'=16] {'fsdp'}, use_global_device_ids=true, to_apply=%region_0.0 | all-reduce | flops 8192 | bytes 65536 | tf_op jit(solution)/shard_map/psum | solution.py:29
  252.6 99.8 %all-reduce.3 = (f32[448,16]{0,1:T(8,128)}, f32[16,128]{1,0:T(8,128)}) all-reduce(f32[448,16]{0,1:T(8,128)S(1)} %convolution_bitcast_fusion.1, f32[16,128]{1,0:T(8,128)S(1)} %fusion.12), channel_id=1, replica_groups=mesh['fsdp'=64,'dp'=16] {'dp'}, use_global_device_ids=true, to_apply=%region_1.0 | all-reduce | flops 9216 | bytes 73728 | tf_op jit(solution)/shard_map/psum | solution.py:56
  352.4 32.6 %while.3 = (s32[]{:T(128)}, bf16[256,448]{0,1:T(8,128)(2,1)}, s32[16,2]{0,1:T(2,128)S(1)}, bf16[16,256,64]{1,2,0:T(8,128)(2,1)S(1)}, s32[]{:T(128)}) while((s32[]{:T(128)}, bf16[256,448]{0,1:T(8,128)(2,1)}, s32[16,2]{0,1:T(2,128)S(1)}, bf16[16,256,64]{1,2,0:T(8,128)(2,1)S(1)}, s32[]{:T(128)}) %tuple.35), condition=%wide.while_cond.1, body=%wide.while_body.1.sunk | while | flops 2 | bytes 65633 | solution.py:36
  353.0 1.4 bitcast_dynamic-update-slice_fusion.5
  355.0 1.4 bitcast_dynamic-update-slice_fusion.5
  357.0 1.4 bitcast_dynamic-update-slice_fusion.5
  359.1 1.4 bitcast_dynamic-update-slice_fusion.5
  361.1 1.4 bitcast_dynamic-update-slice_fusion.5
  365.2 1.4 bitcast_dynamic-update-slice_fusion.5
  373.3 1.4 bitcast_dynamic-update-slice_fusion.5
  379.4 1.4 bitcast_dynamic-update-slice_fusion.5
  385.0 36.2 %while.2 = (s32[]{:T(128)}, bf16[256,8192]{1,0:T(8,128)(2,1)}, s32[16,2]{0,1:T(2,128)S(1)}, bf16[16,256,64]{2,1,0:T(8,128)(2,1)S(1)}, s32[]{:T(128)}) while((s32[]{:T(128)}, bf16[256,8192]{1,0:T(8,128)(2,1)}, s32[16,2]{0,1:T(2,128)S(1)}, bf16[16,256,64]{2,1,0:T(8,128)(2,1)S(1)}, s32[]{:T(128)}) %tuple.32), condition=%wide.while_cond, body=%wide.while_body.sunk | while | flops 2 | bytes 98401 | solution.py:10
  385.6 1.7 bitcast_dynamic-update-slice_fusion.4
  387.9 1.7 bitcast_dynamic-update-slice_fusion.4
  390.1 1.7 bitcast_dynamic-update-slice_fusion.4
  392.4 1.7 bitcast_dynamic-update-slice_fusion.4
  394.6 1.7 bitcast_dynamic-update-slice_fusion.4
  396.9 1.7 bitcast_dynamic-update-slice_fusion.4
  399.2 1.7 bitcast_dynamic-update-slice_fusion.4
  401.4 1.7 bitcast_dynamic-update-slice_fusion.4
  403.7 1.7 bitcast_dynamic-update-slice_fusion.4
  406.0 1.7 bitcast_dynamic-update-slice_fusion.4
  408.2 1.6 bitcast_dynamic-update-slice_fusion.4
  410.4 1.7 bitcast_dynamic-update-slice_fusion.4
  412.7 1.7 bitcast_dynamic-update-slice_fusion.4
  415.0 1.7 bitcast_dynamic-update-slice_fusion.4
  417.2 1.7 bitcast_dynamic-update-slice_fusion.4
  419.5 1.7 bitcast_dynamic-update-slice_fusion.4
  424.8 6.5 %fusion.8 = f32[256,448]{0,1:T(8,128)S(1)} fusion(bf16[256,8192]{1,0:T(8,128)(2,1)} %get-tuple-element.136, bf16[448,8192]{1,0:T(8,128)(2,1)} %param.11), kind=kOutput, calls=%fused_computation.20 | convolution fusion | flops 1879048192 | bytes 11993088 | tf_op jit(solution)/shard_map/dot_general | solution.py:32
  432.5 109.3 %all-reduce.6.cloned.1.call-done = f32[16,64,64]{2,1,0:T(8,128)} async-done(((f32[16,64,64]{2,1,0:T(8,128)}), f32[16,64,64]{2,1,0:T(8,128)}) %all-reduce.6.cloned.1.call-update) | async-done | bytes 262160 | tf_op jit(solution)/shard_map/psum | solution.py:56
  541.8 1.9 copy.37
  (98 shorter events, 40.5 us)
Async XLA Ops:
  7.2 414.0 %copy-start = (f32[16,64,64]{2,1,0:T(8,128)S(1)}, f32[16,64,64]{2,1,0:T(8,128)}, u32[]{:S(2)}) copy-start(f32[16,64,64]{2,1,0:T(8,128)} %param.14) | copy-start | bytes 786436
  7.2 415.2 %copy-start.2 = (s32[16]{0:T(128)S(1)}, s32[16]{0:T(128)}, u32[]{:S(2)}) copy-start(s32[16]{0:T(128)} %param.15) | copy-start | bytes 196
  7.2 377.8 %all-gather.2.cloned.1.call-start = ((), (), s32[]{:S(2)}) async-start(), calls=%async_computation | async-start | bytes 4259840 | tf_op jit(solution)/shard_map/all_gather | solution.py:31
  7.9 533.9 %all-reduce.6.cloned.1.call-start = ((), (), s32[]{:S(2)}) async-start(), calls=%async_computation.1 | async-start | bytes 1048576 | tf_op jit(solution)/shard_map/psum | solution.py:56
  424.8 6.5 %copy-start.1 = (f32[448,16]{0,1:T(8,128)S(1)}, f32[448,16]{0,1:T(8,128)}, u32[]{:S(2)}) copy-start(f32[448,16]{0,1:T(8,128)} %param.12) | copy-start | bytes 86020
Sparse Core Ops, SparseCore 0:
  12.2 106.4 all-gather.1
  424.9 116.8 all-reduce.5
where the time goes:
time: 553 us; the launch traced here: 551 us
  blocking collectives  338 us (61%)
  waiting for transfers between devices  110 us (20%)
  local copies, waits for them, and re-layouts  70.2 us (13%)
  matrix products  15.8 us (3%)
  between operations  14.8 us (3%)
    psum x1, blocking collectives, on_device(): gy_b, h_a = lax.psum((part_gb, part_ha), 'fsdp')  238 us
    psum x1, waiting for transfers between devices, on_device(): lax.psum((local_ga, local_gb, grad_blocks), 'dp')  109 us
    psum x1, blocking collectives, on_device(): lax.psum((local_ga, local_gb, grad_blocks), 'dp')  99.8 us
    gather x96, local copies, waits for them, and re-layouts  68.2 us
  transfers between devices with their start and end apart: 2, of which 1 were waited for; matrix products, arithmetic and copies ran while one was open for 8% of the time, Pallas kernels for 0%

commit v1 on v0

v1 whole, which is shorter than its diff:
```python
import jax
import jax.numpy as jnp
from jax import lax
from jax.experimental import pallas as pl
from jax.experimental.pallas import tpu as pltpu
from jax.sharding import PartitionSpec as P

MESH = pl.DeviceIdType.MESH
BF16, F32 = jnp.bfloat16, jnp.float32
HIGHEST = lax.Precision.HIGHEST
OFFSETS = (0, 1, -1, 2, -2, 3, -3, 4)
CHUNKS = ((0, 1, 0), (1, 2, 1), (3, 2, 2), (5, 2, 3), (7, 1, 4))
BOTH = tuple((half, way) for way in (0, 1) for half in (0, 1))
STEP = (1, -1)
HOP = {1: 1, 2: 2, 3: 1, 4: 2}


def ring_slot(step, distance):
    if distance in (0, 4):
        return 0 if distance == 0 else 7
    return 2 * distance - 1 if step == -1 else 2 * distance


def slot_of(offset):
    return jnp.where(offset == 0, 0, jnp.where(offset <= 4, 2 * offset - 1, 16 - 2 * offset))


def nt(a, b):
    return lax.dot_general(a, b, (((1,), (1,)), ((), ())), preferred_element_type=F32)


def nn(a, b):
    return lax.dot_general(a, b, (((1,), (0,)), ((), ())), preferred_element_type=F32)


def pieces(value):
    first = value.astype(BF16)
    rest = value - first.astype(F32)
    second = rest.astype(BF16)
    third = (rest - second.astype(F32)).astype(BF16)
    return first, second, third


def exact(product, value, other):
    return sum(product(piece, other) for piece in pieces(value)[::-1])


def kernel(
    gy_hbm, ht_hbm, w_hbm, at_hbm, b_hbm, vals_hbm, row_ref, col_ref, count_ref,
    gh_out, ga_out, gb_out, gd_out,
    buf, gy_v, ht_v, w_v, at_v, b_v, vals_v, load_sem,
    acc, spread, chosen,
    ring_send, ring_recv, bulk_send, bulk_recv,
    small, small_1, small_2, small_3, small_all, small_send, small_recv,
    sums, sums_core, sums_half, sums_y, sums_all, sums_send, sums_recv,
):
    f = lax.axis_index("fsdp")
    d = lax.axis_index("dp")
    x, z, y, core = f // 8, f % 8, d // 2, d % 2

    def along_x(k):
        return ((x + k + 8) % 8 * 8 + z, d)

    def along_z(k):
        return (x * 8 + (z + k + 8) % 8, d)

    def along_y(k):
        return (f, (y + k + 8) % 8 * 2 + core)

    other_core = (f, y * 2 + 1 - core)

    def first_axis(half, k):
        return along_z(k) if half else along_x(k)

    def second_axis(half, k):
        return along_x(k) if half else along_z(k)

    barrier = pltpu.get_barrier_semaphore()
    peers = [way(k) for way in (along_x, along_z, along_y) for k in range(1, 8)] + [other_core]
    for peer in peers:
        pl.semaphore_signal(barrier, inc=1, device_id=peer, device_id_type=MESH)

    loads = {
        "gy0": pltpu.make_async_copy(gy_hbm.at[pl.ds(0, 128)], buf.at[0, 0, 0], load_sem.at[0]),
        "gy1": pltpu.make_async_copy(gy_hbm.at[pl.ds(128, 128)], buf.at[1, 0, 0], load_sem.at[1]),
        "gy": pltpu.make_async_copy(gy_hbm, gy_v, load_sem.at[2]),
        "ht": pltpu.make_async_copy(ht_hbm, ht_v, load_sem.at[3]),
        "at": pltpu.make_async_copy(at_hbm, at_v, load_sem.at[4]),
        "b": pltpu.make_async_copy(b_hbm, b_v, load_sem.at[5]),
        "vals": pltpu.make_async_copy(vals_hbm, vals_v, load_sem.at[6]),
        "w": pltpu.make_async_copy(w_hbm, w_v, load_sem.at[7]),
    }
    for load in loads.values():
        load.start()
    loads["gy0"].wait()
    loads["gy1"].wait()
    pl.semaphore_wait(barrier, len(peers))

    sent = []

    def send(copy):
        copy.start()
        sent.append(copy)

    def ring(half, way, distance):
        step = STEP[way]
        source, target = ring_slot(step, distance - HOP[distance]), ring_slot(step, distance)
        rows = pl.ds(0, 128) if distance < 4 else pl.ds(way * 64, 64)
        return pltpu.make_async_remote_copy(
            buf.at[half, source, 0, rows], buf.at[half, target, 0, rows],
            ring_send.at[half, way, distance - 1], ring_recv.at[half, way, distance - 1],
            device_id=first_axis(half, step * HOP[distance]), device_id_type=MESH,
        )

    def bulk(half, way, hop, chunk):
        step = STEP[way]
        source, target = ring_slot(step, hop), ring_slot(step, hop + 1)
        rows = pl.ds(0, 128) if hop < 3 else pl.ds(way * 64, 64)
        slots = pl.ds(CHUNKS[chunk][0], CHUNKS[chunk][1])
        return pltpu.make_async_remote_copy(
            buf.at[half, slots, source, rows], buf.at[half, slots, target, rows],
            bulk_send.at[half, way, hop, chunk], bulk_recv.at[half, way, hop, chunk],
            device_id=second_axis(half, step), device_id_type=MESH,
        )

    def ring_arrive(distance):
        for half, way in BOTH:
            ring(half, way, distance).wait_recv()
            for later in (3, 4):
                if later - HOP[later] == distance:
                    send(ring(half, way, later))
        for chunk, entry in enumerate(CHUNKS):
            if entry[2] == distance:
                for half, way in BOTH:
                    send(bulk(half, way, 0, chunk))

    def bulk_arrive(hop, chunk):
        for half, way in BOTH:
            bulk(half, way, hop, chunk).wait_recv()
            if hop < 3:
                send(bulk(half, way, hop + 1, chunk))

    def dense(half, slot):
        across = OFFSETS[slot]
        weight, blocks = [], []
        for other in range(8):
            along = OFFSETS[other]
            if half == 0:
                owner = (x + along + 8) % 8 * 8 + (z + across + 8) % 8
            else:
                owner = (x + across + 8) % 8 * 8 + (z + along + 8) % 8
            weight.append(w_v[:, pl.ds(pl.multiple_of(owner * 128, 128), 128)])
            blocks.append(buf[half, other, slot])
        part = nt(jnp.concatenate(weight, axis=1), jnp.concatenate(blocks, axis=1))
        place = pl.ds(half * 128, 128)
        acc[:, place] = part if slot == 0 else acc[:, place] + part

    def small_copy(stage, k):
        source, target, peer = (
            (small.at[(x + k) % 8], small_1.at[k], along_x(k)),
            (small_2.at[0], small_2.at[k], along_z(k)),
            (small_3.at[0], small_3.at[k], along_x(k)),
        )[stage]
        return pltpu.make_async_remote_copy(
            source, target, small_send.at[stage, k], small_recv.at[stage, k],
            device_id=peer, device_id_type=MESH,
        )

    def small_start():
        for name in ("gy", "ht", "at", "b"):
            loads[name].wait()
        part_gb = exact(nt, b_v[...], gy_v[...])
        part_ha = exact(nn, at_v[...], ht_v[...].reshape(448, 256))
        for piece in range(8):
            group, side = piece // 2, piece % 2
            source = part_gb if group < 2 else part_ha
            small[piece] = source[group % 2 * 8 : group % 2 * 8 + 8, side * 128 : side * 128 + 128]
        for k in range(1, 8):
            send(small_copy(0, k))

    def small_second():
        for k in range(1, 8):
            small_copy(0, k).wait_recv()
        total = small[x]
        for k in range(1, 8):
            total = total + small_1[k]
        small_2[0] = total
        for k in range(1, 8):
            send(small_copy(1, k))

    def small_third():
        for k in range(1, 8):
            small_copy(1, k).wait_recv()
        total = small_2[0]
        for k in range(1, 8):
            total = total + small_2[k]
        small_3[0] = total
        for k in range(1, 8):
            send(small_copy(2, k))

    def small_end():
        small_all[x] = small_3[0]
        for k in range(1, 8):
            small_copy(2, k).wait_recv()
            small_all[(x + 8 - k) % 8] = small_3[k]
        rows = [
            jnp.concatenate([small_all[2 * group], small_all[2 * group + 1]], axis=1)
            for group in range(4)
        ]
        gy_b = jnp.concatenate(rows[:2], axis=0)
        h_a = jnp.concatenate(rows[2:], axis=0)
        grad_a = exact(nt, gy_b, ht_v[...].reshape(448, 256))
        grad_b = exact(nn, h_a, gy_v[...])
        wide = jnp.concatenate([grad_a, jnp.zeros((16, 64), F32), grad_b], axis=1)
        for tile in range(16):
            if tile < 10:
                group, lane = tile // 5, tile % 5 * 128
                value = wide[group * 8 : group * 8 + 8, lane : lane + 128]
            else:
                value = jnp.zeros((8, 128), F32)
            sums[tile // 2, tile % 2, 32:40] = value
        adapter = lax.dot_general(
            at_v[...], gy_b, (((0,), (0,)), ((), ())), precision=HIGHEST,
            preferred_element_type=F32,
        )
        acc[...] += adapter

    def spread_deltas():
        loads["vals"].wait()
        live_slots = count_ref[0]
        side = lax.broadcasted_iota(jnp.int32, (64, 128), 1) // 64
        for k in range(16):
            value = vals_v[k]
            keep = (side == col_ref[k] % 2) & (live_slots > k)
            value = jnp.where(keep, jnp.concatenate([value, value], axis=1), 0.0)
            first, second, _ = pieces(value)
            place = pl.ds(k * 128, 128)
            for block in range(7):
                here = row_ref[k] == block
                rows = pl.ds(block * 64, 64)
                spread[0, rows, place] = jnp.where(here, first, jnp.zeros_like(first))
                spread[1, rows, place] = jnp.where(here, second, jnp.zeros_like(second))

    def choose():
        for k in range(16):
            owner = col_ref[k] // 2
            slot_x = slot_of((owner // 8 - x + 8) % 8)
            slot_z = slot_of((owner % 8 - z + 8) % 8)
            place = pl.ds(k * 128, 128)
            chosen[0:128, place] = buf[0, slot_x, slot_z]
            chosen[128:256, place] = buf[1, slot_z, slot_x]

    def grad_deltas():
        live_slots = count_ref[0]
        lane = lax.broadcasted_iota(jnp.int32, (64, 128), 1)
        for pair in range(8):
            sides = []
            for k in (pair, pair + 8):
                block = nn(ht_v[row_ref[k]], chosen[:, k * 128 : k * 128 + 128])
                block = jnp.where(live_slots > k, block, 0.0)
                swap = (col_ref[k] % 2) != (k // 8)
                sides.append(jnp.where(swap, pltpu.roll(block, 64, 1), block))
            both = jnp.where(lane < 64, sides[0], sides[1])
            sums[pair, 0, 0:32] = both[0:32]
            sums[pair, 1, 0:32] = both[32:64]

    def sums_copy(stage, k):
        source, target, peer = (
            lambda: (sums.at[:, 1 - core], sums_core, other_core),
            lambda: (sums_half.at[(y + k) % 8], sums_y.at[k], along_y(k)),
            lambda: (sums_all.at[y, core], sums_all.at[y, core], along_y(k)),
            lambda: (sums_all.at[(y + 8 - k) % 8, core], sums_all.at[(y + 8 - k) % 8, core], other_core),
        )[stage]()
        return pltpu.make_async_remote_copy(
            source, target, sums_send.at[stage, k], sums_recv.at[stage, k],
            device_id=peer, device_id_type=MESH,
        )

    for half, way in BOTH:
        send(ring(half, way, 1))
    for half, way in BOTH:
        send(bulk(half, way, 0, 0))
    for half, way in BOTH:
        send(ring(half, way, 2))
    small_start()

    ring_arrive(1)
    ring_arrive(2)
    bulk_arrive(0, 0)
    small_second()

    ring_arrive(3)
    ring_arrive(4)
    bulk_arrive(1, 0)
    bulk_arrive(0, 1)
    bulk_arrive(0, 2)
    small_third()
    loads["w"].wait()
    dense(0, 0)
    dense(1, 0)

    for wave in range(2, 6):
        for chunk in range(5):
            hop = wave - (0, 1, 1, 2, 2)[chunk]
            if hop < 4:
                bulk_arrive(hop, chunk)
        if wave == 2:
            small_end()
            spread_deltas()
        hop = wave - 2
        if hop < 3:
            for half, way in BOTH:
                dense(half, ring_slot(STEP[way], hop + 1))

    choose()
    grad_deltas()
    send(sums_copy(0, 0))
    dense(0, 7)
    dense(1, 7)
    sums_copy(0, 0).wait_recv()
    sums_half[...] = sums[:, core] + sums_core[...]
    for k in range(1, 8):
        send(sums_copy(1, k))
    total = acc[...]
    for part in (1, 0):
        total = total + nt(spread[part], chosen[...])
    gh_out[...] = total.astype(BF16)
    total = sums_half[y]
    for k in range(1, 8):
        sums_copy(1, k).wait_recv()
        total = total + sums_y[k]
    sums_all[y, core] = total
    for k in range(1, 8):
        send(sums_copy(2, k))
    send(sums_copy(3, 0))
    for k in range(1, 8):
        sums_copy(2, k).wait_recv()
        send(sums_copy(3, k))
    for k in range(8):
        sums_copy(3, k).wait_recv()
    for pair in range(8):
        for side in (0, 1):
            value = sums_all[pair, side]
            rows = pl.ds(side * 32, 32)
            gd_out[pair, rows] = value[0:32, 0:64]
            gd_out[pair + 8, rows] = value[0:32, 64:128]
            tile = 2 * pair + side
            if tile < 10:
                group, lane = pl.ds(tile // 5 * 8, 8), tile % 5
                if lane < 3:
                    ga_out[group, lane * 128 : lane * 128 + 128] = value[32:40]
                elif lane == 3:
                    ga_out[group, 384:448] = value[32:40, 0:64]
                else:
                    gb_out[group, :] = value[32:40]
    for copy in sent:
        copy.wait_send()


def on_device(
    grad_out, hidden, base_weight, adapt_a, adapt_b, delta_vals, blk_row, blk_col, blk_count
):
    hbm = pl.BlockSpec(memory_space=pltpu.HBM)
    scalar = pl.BlockSpec(memory_space=pltpu.SMEM)
    vmem = pl.BlockSpec(memory_space=pltpu.VMEM)
    dma = pltpu.SemaphoreType.DMA
    gh, ga, gb, gd = pl.pallas_call(
        kernel,
        out_shape=(
            jax.ShapeDtypeStruct((448, 256), BF16),
            jax.ShapeDtypeStruct((16, 448), F32),
            jax.ShapeDtypeStruct((16, 128), F32),
            jax.ShapeDtypeStruct((16, 64, 64), F32),
        ),
        in_specs=[hbm] * 6 + [scalar] * 3,
        out_specs=(vmem,) * 4,
        scratch_shapes=[
            pltpu.VMEM((2, 8, 8, 128, 128), BF16),
            pltpu.VMEM((256, 128), BF16),
            pltpu.VMEM((7, 64, 256), BF16),
            pltpu.VMEM((448, 8192), BF16),
            pltpu.VMEM((16, 448), F32),
            pltpu.VMEM((16, 128), F32),
            pltpu.VMEM((16, 64, 64), F32),
            dma((8,)),
            pltpu.VMEM((448, 256), F32),
            pltpu.VMEM((2, 448, 2048), BF16),
            pltpu.VMEM((256, 2048), BF16),
            dma((2, 2, 4)),
            dma((2, 2, 4)),
            dma((2, 2, 4, 5)),
            dma((2, 2, 4, 5)),
            pltpu.VMEM((8, 8, 128), F32),
            pltpu.VMEM((8, 8, 128), F32),
            pltpu.VMEM((8, 8, 128), F32),
            pltpu.VMEM((8, 8, 128), F32),
            pltpu.VMEM((8, 8, 128), F32),
            dma((3, 8)),
            dma((3, 8)),
            pltpu.VMEM((8, 2, 40, 128), F32),
            pltpu.VMEM((8, 40, 128), F32),
            pltpu.VMEM((8, 40, 128), F32),
            pltpu.VMEM((8, 40, 128), F32),
            pltpu.VMEM((8, 2, 40, 128), F32),
            dma((4, 8)),
            dma((4, 8)),
        ],
        compiler_params=pltpu.CompilerParams(
            collective_id=0, has_side_effects=True, vmem_limit_bytes=60 << 20
        ),
        cost_estimate=pl.CostEstimate(
            flops=3_000_000_000, bytes_accessed=12_000_000, transcendentals=0
        ),
    )(
        grad_out, hidden.T.reshape(7, 64, 256), base_weight, adapt_a.T, adapt_b, delta_vals,
        blk_row, blk_col, blk_count,
    )
    return gh.T, ga.T, gb, gd


def solution(mesh):
    placed = (
        P("dp", "fsdp"),
        P("dp", "fsdp"),
        P("fsdp", None),
        P("fsdp", None),
        P(None, "fsdp"),
        P("fsdp", None, None),
        P("fsdp"),
        P("fsdp"),
        P("fsdp"),
    )
    return jax.shard_map(
        on_device,
        mesh=mesh,
        in_specs=placed,
        out_specs=(P("dp", "fsdp"), P("fsdp", None), P(None, "fsdp"), P("fsdp", None, None)),
        check_vma=False,
    )
```

time: 553 us -> 85.9 us (0.16)
  blocking collectives: 338 us -> 0 us
  waiting for transfers between devices: 110 us -> 0 us
  Pallas kernels: 0 us -> 78 us
  local copies, waits for them, and re-layouts: 70.2 us -> 6.19 us
  matrix products: 15.8 us -> 0 us
  between operations: 14.8 us -> 1.29 us
    psum x2 -> x0, blocking collectives: 338 us -> none  [the longest x1 238 us: on_device(): gy_b, h_a = lax.psum((part_gb, part_ha), 'fsdp')]
    psum x1 -> x0, waiting for transfers between devices: 109 us -> none  [on_device(): lax.psum((local_ga, local_gb, grad_blocks), 'dp')]
    pallas_call x0 -> x1, Pallas kernels: none -> 78 us  [on_device(): pl.pallas_call(kernel, out_shape=(jax.ShapeDtypeStruct((448, 256), BF16),...]
    gather x96 -> x0, local copies, waits for them, and re-layouts: 68.2 us -> none
    dot_general x9 -> x0, matrix products: 15.8 us -> none  [the longest x1 6.45 us: on_device(): dense = jnp.dot(gy_full, base_weight.T, preferred_element_type=jnp.float32)]
  transfers between devices with their start and end apart: 2 -> 0, of which waited for: 1 -> 0; matrix products, arithmetic and copies ran while one was open for 8% -> 0% of each run, Pallas kernels for 0% -> 0%
where the time goes in v1:
time: 85.9 us; the launch traced here: 85.5 us
  Pallas kernels  78 us (91%)
  local copies, waits for them, and re-layouts  6.19 us (7%)
  between operations  1.29 us (2%)
    pallas_call x1, Pallas kernels, on_device(): pl.pallas_call(kernel, out_shape=(jax.ShapeDtypeStruct((448, 256), BF16),...  78 us
    unnamed x4, local copies, waits for them, and re-layouts  6.19 us

profile of v1, /device:TPU:1, one launch (start us, length us, event | category | flops | bytes accessed | tf_op | source)
XLA Modules:
  0.0 85.5 jit_solution(7361165073142013394)
XLA Ops:
  1.3 78.0 %shard_map.120 = (bf16[448,256]{1,0:T(8,128)(2,1)}, f32[16,448]{1,0:T(8,128)}, f32[16,128]{1,0:T(8,128)}, f32[16,64,64]{2,1,0:T(8,128)}) custom-call(bf16[256,128]{1,0:T(8,128)(2,1)} %gy_hbm.1, bf16[7,64,256]{2,1,0:T(8,128)(2,1)} %bitcast.8, bf16[448,8192]{1,0:T(8,128)(2,1)} %w_hbm.1, f32[16,448]{1,0:T(8,128)} %bitcast.9, f32[16,128]{1,0:T(8,128)} %b_hbm.1, ...), custom_call_target="tpu_custom_call" | custom-call | flops 3000000000 | bytes 12000000 | tf_op jit(solution)/shard_map/pallas_call | solution.py:367
  79.3 1.6 %copy.18 = bf16[256,448]{0,1:T(8,128)(2,1)} copy(bf16[256,448]{0,1:T(8,128)(2,1)} %bitcast.6) | data formatting | bytes 458752
  81.0 1.4 %copy.19 = f32[448,16]{0,1:T(8,128)} copy(f32[448,16]{0,1:T(8,128)} %bitcast.7) | data formatting | bytes 57344
  82.3 1.3 %copy.20 = f32[16,128]{1,0:T(8,128)} copy(f32[16,128]{1,0:T(8,128)} %get-tuple-element.18) | data formatting | bytes 16384
  83.6 1.9 %copy.21 = f32[16,64,64]{2,1,0:T(8,128)} copy(f32[16,64,64]{2,1,0:T(8,128)} %get-tuple-element.19) | data formatting | bytes 524288

commit v2 on v1

--- a/solution.py
+++ b/solution.py
@@ -47,9 +47,9 @@
 
 def kernel(
     gy_hbm, ht_hbm, w_hbm, at_hbm, b_hbm, vals_hbm, row_ref, col_ref, count_ref,
-    gh_out, ga_out, gb_out, gd_out,
+    gh_out, sums_out,
     buf, gy_v, ht_v, w_v, at_v, b_v, vals_v, load_sem,
-    acc, spread, chosen,
+    acc, spread, chosen, gh_v,
     ring_send, ring_recv, bulk_send, bulk_recv,
     small, small_1, small_2, small_3, small_all, small_send, small_recv,
     sums, sums_core, sums_half, sums_y, sums_all, sums_send, sums_recv,
@@ -287,14 +287,13 @@
     ring_arrive(1)
     ring_arrive(2)
     bulk_arrive(0, 0)
-    small_second()
 
     ring_arrive(3)
     ring_arrive(4)
     bulk_arrive(1, 0)
     bulk_arrive(0, 1)
     bulk_arrive(0, 2)
-    small_third()
+    small_second()
     loads["w"].wait()
     dense(0, 0)
     dense(1, 0)
@@ -305,26 +304,31 @@
             if hop < 4:
                 bulk_arrive(hop, chunk)
         if wave == 2:
-            small_end()
             spread_deltas()
+        if wave == 3:
+            small_third()
         hop = wave - 2
         if hop < 3:
             for half, way in BOTH:
                 dense(half, ring_slot(STEP[way], hop + 1))
+        if wave == 4:
+            small_end()
 
     choose()
     grad_deltas()
     send(sums_copy(0, 0))
-    dense(0, 7)
-    dense(1, 7)
     sums_copy(0, 0).wait_recv()
     sums_half[...] = sums[:, core] + sums_core[...]
     for k in range(1, 8):
         send(sums_copy(1, k))
+    dense(0, 7)
+    dense(1, 7)
     total = acc[...]
     for part in (1, 0):
         total = total + nt(spread[part], chosen[...])
-    gh_out[...] = total.astype(BF16)
+    gh_v[...] = total.astype(BF16)
+    gh_copy = pltpu.make_async_copy(gh_v, gh_out, load_sem.at[0])
+    gh_copy.start()
     total = sums_half[y]
     for k in range(1, 8):
         sums_copy(1, k).wait_recv()
@@ -338,9 +342,19 @@
         send(sums_copy(3, k))
     for k in range(8):
         sums_copy(3, k).wait_recv()
+    sums_write = pltpu.make_async_copy(sums_all, sums_out, load_sem.at[1])
+    sums_write.start()
+    for copy in sent:
+        copy.wait_send()
+    gh_copy.wait()
+    sums_write.wait()
+
+
+def finish(gh_in, sums_in, gh_out, ga_out, gb_out, gd_out):
+    gh_out[...] = gh_in[...]
     for pair in range(8):
         for side in (0, 1):
-            value = sums_all[pair, side]
+            value = sums_in[pair, side]
             rows = pl.ds(side * 32, 32)
             gd_out[pair, rows] = value[0:32, 0:64]
             gd_out[pair + 8, rows] = value[0:32, 64:128]
@@ -353,8 +367,6 @@
                     ga_out[group, 384:448] = value[32:40, 0:64]
                 else:
                     gb_out[group, :] = value[32:40]
-    for copy in sent:
-        copy.wait_send()
 
 
 def on_device(
@@ -364,16 +376,15 @@
     scalar = pl.BlockSpec(memory_space=pltpu.SMEM)
     vmem = pl.BlockSpec(memory_space=pltpu.VMEM)
     dma = pltpu.SemaphoreType.DMA
-    gh, ga, gb, gd = pl.pallas_call(
+    small_tiles = pltpu.VMEM((8, 8, 128), F32)
+    gathered, summed = pl.pallas_call(
         kernel,
         out_shape=(
             jax.ShapeDtypeStruct((448, 256), BF16),
-            jax.ShapeDtypeStruct((16, 448), F32),
-            jax.ShapeDtypeStruct((16, 128), F32),
-            jax.ShapeDtypeStruct((16, 64, 64), F32),
+            jax.ShapeDtypeStruct((8, 2, 40, 128), F32),
         ),
         in_specs=[hbm] * 6 + [scalar] * 3,
-        out_specs=(vmem,) * 4,
+        out_specs=(hbm, hbm),
         scratch_shapes=[
             pltpu.VMEM((2, 8, 8, 128, 128), BF16),
             pltpu.VMEM((256, 128), BF16),
@@ -386,15 +397,16 @@
             pltpu.VMEM((448, 256), F32),
             pltpu.VMEM((2, 448, 2048), BF16),
             pltpu.VMEM((256, 2048), BF16),
+            pltpu.VMEM((448, 256), BF16),
             dma((2, 2, 4)),
             dma((2, 2, 4)),
             dma((2, 2, 4, 5)),
             dma((2, 2, 4, 5)),
-            pltpu.VMEM((8, 8, 128), F32),
-            pltpu.VMEM((8, 8, 128), F32),
-            pltpu.VMEM((8, 8, 128), F32),
-            pltpu.VMEM((8, 8, 128), F32),
-            pltpu.VMEM((8, 8, 128), F32),
+            small_tiles,
+            small_tiles,
+            small_tiles,
+            small_tiles,
+            small_tiles,
             dma((3, 8)),
             dma((3, 8)),
             pltpu.VMEM((8, 2, 40, 128), F32),
@@ -415,6 +427,18 @@
         grad_out, hidden.T.reshape(7, 64, 256), base_weight, adapt_a.T, adapt_b, delta_vals,
         blk_row, blk_col, blk_count,
     )
+    gh, ga, gb, gd = pl.pallas_call(
+        finish,
+        out_shape=(
+            jax.ShapeDtypeStruct((448, 256), BF16),
+            jax.ShapeDtypeStruct((16, 448), F32),
+            jax.ShapeDtypeStruct((16, 128), F32),
+            jax.ShapeDtypeStruct((16, 64, 64), F32),
+        ),
+        in_specs=[vmem] * 2,
+        out_specs=(vmem,) * 4,
+        compiler_params=pltpu.CompilerParams(vmem_limit_bytes=60 << 20),
+    )(gathered, summed)
     return gh.T, ga.T, gb, gd
 
 

time: 85.9 us -> 78.7 us (0.916)
  the two profiles are of different devices: /device:TPU:1 before, /device:TPU:5 now
where the time goes in v2:
time: 78.7 us; the launch traced here: 78.5 us
  Pallas kernels  77.2 us (98%)
  between operations  1.29 us (2%)
    pallas_call x1, Pallas kernels, on_device(): pl.pallas_call(kernel, out_shape=(jax.ShapeDtypeStruct((448, 256), BF16),...  75.2 us
    pallas_call x1, Pallas kernels, on_device(): pl.pallas_call(finish, out_shape=(jax.ShapeDtypeStruct((448, 256), BF16),...  2.03 us

profile of v2, /device:TPU:5, one launch (start us, length us, event | category | flops | bytes accessed | tf_op | source)
XLA Modules:
  0.0 78.5 jit_solution(9488230263206265423)
XLA Ops:
  1.3 75.2 %shard_map.120 = (bf16[448,256]{1,0:T(8,128)(2,1)}, f32[8,2,40,128]{3,2,1,0:T(8,128)}) custom-call(bf16[256,128]{1,0:T(8,128)(2,1)} %gy_hbm.1, bf16[7,64,256]{2,1,0:T(8,128)(2,1)} %bitcast.6, bf16[448,8192]{1,0:T(8,128)(2,1)} %w_hbm.1, f32[16,448]{1,0:T(8,128)} %bitcast.8, f32[16,128]{1,0:T(8,128)} %b_hbm.1, f32[16,64,64]{2,1,0:T(8,128)} %vals_hbm.1, ...), custom_call_target="tpu_custom_call" | custom-call | flops 3000000000 | bytes 12000000 | tf_op jit(solution)/shard_map/pallas_call | solution.py:380
  76.5 2.0 %shard_map.121 = (bf16[448,256]{1,0:T(8,128)(2,1)}, f32[16,448]{1,0:T(8,128)}, f32[16,128]{1,0:T(8,128)}, f32[16,64,64]{2,1,0:T(8,128)}) custom-call(bf16[448,256]{1,0:T(8,128)(2,1)} %get-tuple-element.10.gh_in, f32[8,2,40,128]{3,2,1,0:T(8,128)} %get-tuple-element.11.sums_in), custom_call_target="tpu_custom_call" | custom-call | tf_op jit(solution)/shard_map/pallas_call | solution.py:430

commit v3 on v2

--- a/solution.py
+++ b/solution.py
@@ -12,6 +12,7 @@
 CHUNKS = ((0, 1, 0), (1, 2, 1), (3, 2, 2), (5, 2, 3), (7, 1, 4))
 BOTH = tuple((half, way) for way in (0, 1) for half in (0, 1))
 STEP = (1, -1)
+FAR_FIRST = (4, 3, 5, 2, 6, 1, 7)
 HOP = {1: 1, 2: 2, 3: 1, 4: 2}
 
 
@@ -50,7 +51,7 @@
     gh_out, sums_out,
     buf, gy_v, ht_v, w_v, at_v, b_v, vals_v, load_sem,
     acc, spread, chosen, gh_v,
-    ring_send, ring_recv, bulk_send, bulk_recv,
+    ring_send, ring_recv, bulk_send, bulk_recv, ready, ready_core,
     small, small_1, small_2, small_3, small_all, small_send, small_recv,
     sums, sums_core, sums_half, sums_y, sums_all, sums_send, sums_recv,
 ):
@@ -75,10 +76,19 @@
     def second_axis(half, k):
         return along_x(k) if half else along_z(k)
 
+    def at_z(other):
+        return (x * 8 + other, d)
+
+    def signal(semaphore, peer):
+        pl.semaphore_signal(semaphore, inc=1, device_id=peer, device_id_type=MESH)
+
     barrier = pltpu.get_barrier_semaphore()
-    peers = [way(k) for way in (along_x, along_z, along_y) for k in range(1, 8)] + [other_core]
-    for peer in peers:
-        pl.semaphore_signal(barrier, inc=1, device_id=peer, device_id_type=MESH)
+    for k in range(1, 8):
+        signal(barrier, along_x(k))
+        pl.when(z < k)(lambda k=k: signal(barrier, at_z(k)))
+    for k in range(1, 8):
+        signal(barrier, along_y(k))
+    pl.when(core == 0)(lambda: signal(barrier, other_core))
 
     loads = {
         "gy0": pltpu.make_async_copy(gy_hbm.at[pl.ds(0, 128)], buf.at[0, 0, 0], load_sem.at[0]),
@@ -94,7 +104,10 @@
         load.start()
     loads["gy0"].wait()
     loads["gy1"].wait()
-    pl.semaphore_wait(barrier, len(peers))
+    pl.semaphore_wait(barrier, 14 + z + core)
+    for k in range(7):
+        pl.when(z > k)(lambda k=k: signal(ready.at[z], at_z(k)))
+    pl.when(core == 1)(lambda: signal(ready_core, other_core))
 
     sent = []
 
@@ -175,7 +188,7 @@
             group, side = piece // 2, piece % 2
             source = part_gb if group < 2 else part_ha
             small[piece] = source[group % 2 * 8 : group % 2 * 8 + 8, side * 128 : side * 128 + 128]
-        for k in range(1, 8):
+        for k in FAR_FIRST:
             send(small_copy(0, k))
 
     def small_second():
@@ -185,7 +198,10 @@
         for k in range(1, 8):
             total = total + small_1[k]
         small_2[0] = total
-        for k in range(1, 8):
+        for k in range(3, 8):
+            opened = (k <= z + 2) | (k >= z + 6)
+            pl.when(jnp.logical_not(opened))(lambda k=k: pl.semaphore_wait(ready.at[k], 1))
+        for k in FAR_FIRST:
             send(small_copy(1, k))
 
     def small_third():
@@ -195,7 +211,7 @@
         for k in range(1, 8):
             total = total + small_2[k]
         small_3[0] = total
-        for k in range(1, 8):
+        for k in FAR_FIRST:
             send(small_copy(2, k))
 
     def small_end():
@@ -276,13 +292,36 @@
             device_id=peer, device_id_type=MESH,
         )
 
-    for half, way in BOTH:
-        send(ring(half, way, 1))
-    for half, way in BOTH:
-        send(bulk(half, way, 0, 0))
-    for half, way in BOTH:
-        send(ring(half, way, 2))
+    for way in (0, 1):
+        send(ring(0, way, 1))
+    for way in (0, 1):
+        send(bulk(1, way, 0, 0))
+    for way in (0, 1):
+        send(ring(0, way, 2))
+    to_z = {
+        1: [ring(1, 0, 1), bulk(0, 0, 0, 0)],
+        2: [ring(1, 0, 2)],
+        -1: [ring(1, 1, 1), bulk(0, 1, 0, 0)],
+        -2: [ring(1, 1, 2)],
+    }
+
+    def open_z(offset, wait):
+        if wait:
+            pl.semaphore_wait(ready.at[(z + offset + 8) % 8], 1)
+        for copy in to_z[offset]:
+            copy.start()
+
+    for copies in to_z.values():
+        sent.extend(copies)
+    pl.when(z >= 1)(lambda: open_z(-1, False))
+    pl.when(z >= 2)(lambda: open_z(-2, False))
+    pl.when(z >= 7)(lambda: open_z(1, False))
+    pl.when(z >= 6)(lambda: open_z(2, False))
     small_start()
+    pl.when(z < 7)(lambda: open_z(1, True))
+    pl.when(z < 6)(lambda: open_z(2, True))
+    pl.when(z < 2)(lambda: open_z(-2, True))
+    pl.when(z < 1)(lambda: open_z(-1, True))
 
     ring_arrive(1)
     ring_arrive(2)
@@ -316,10 +355,11 @@
 
     choose()
     grad_deltas()
+    pl.when(core == 0)(lambda: pl.semaphore_wait(ready_core, 1))
     send(sums_copy(0, 0))
     sums_copy(0, 0).wait_recv()
     sums_half[...] = sums[:, core] + sums_core[...]
-    for k in range(1, 8):
+    for k in FAR_FIRST:
         send(sums_copy(1, k))
     dense(0, 7)
     dense(1, 7)
@@ -334,10 +374,10 @@
         sums_copy(1, k).wait_recv()
         total = total + sums_y[k]
     sums_all[y, core] = total
-    for k in range(1, 8):
+    for k in FAR_FIRST:
         send(sums_copy(2, k))
     send(sums_copy(3, 0))
-    for k in range(1, 8):
+    for k in FAR_FIRST[::-1]:
         sums_copy(2, k).wait_recv()
         send(sums_copy(3, k))
     for k in range(8):
@@ -402,6 +442,8 @@
             dma((2, 2, 4)),
             dma((2, 2, 4, 5)),
             dma((2, 2, 4, 5)),
+            pltpu.SemaphoreType.REGULAR((8,)),
+            pltpu.SemaphoreType.REGULAR,
             small_tiles,
             small_tiles,
             small_tiles,

time: 78.7 us -> 78.9 us (level)
  the two profiles are of different devices: /device:TPU:5 before, /device:TPU:1 now
where the time goes in v3:
time: 78.9 us; the launch traced here: 78.7 us
  Pallas kernels  77.4 us (98%)
  between operations  1.29 us (2%)
    pallas_call x1, Pallas kernels, on_device(): pl.pallas_call(kernel, out_shape=(jax.ShapeDtypeStruct((448, 256), BF16),...  75.4 us
    pallas_call x1, Pallas kernels, on_device(): pl.pallas_call(finish, out_shape=(jax.ShapeDtypeStruct((448, 256), BF16),...  2.03 us

profile of v3, /device:TPU:1, one launch (start us, length us, event | category | flops | bytes accessed | tf_op | source)
XLA Modules:
  0.0 78.7 jit_solution(4061967629463931071)
XLA Ops:
  1.3 75.4 %shard_map.120 = (bf16[448,256]{1,0:T(8,128)(2,1)}, f32[8,2,40,128]{3,2,1,0:T(8,128)}) custom-call(bf16[256,128]{1,0:T(8,128)(2,1)} %gy_hbm.1, bf16[7,64,256]{2,1,0:T(8,128)(2,1)} %bitcast.6, bf16[448,8192]{1,0:T(8,128)(2,1)} %w_hbm.1, f32[16,448]{1,0:T(8,128)} %bitcast.8, f32[16,128]{1,0:T(8,128)} %b_hbm.1, f32[16,64,64]{2,1,0:T(8,128)} %vals_hbm.1, ...), custom_call_target="tpu_custom_call" | custom-call | flops 3000000000 | bytes 12000000 | tf_op jit(solution)/shard_map/pallas_call | solution.py:420
  76.7 2.0 %shard_map.121 = (bf16[448,256]{1,0:T(8,128)(2,1)}, f32[16,448]{1,0:T(8,128)}, f32[16,128]{1,0:T(8,128)}, f32[16,64,64]{2,1,0:T(8,128)}) custom-call(bf16[448,256]{1,0:T(8,128)(2,1)} %get-tuple-element.10.gh_in, f32[8,2,40,128]{3,2,1,0:T(8,128)} %get-tuple-element.11.sums_in), custom_call_target="tpu_custom_call" | custom-call | tf_op jit(solution)/shard_map/pallas_call | solution.py:472

commit v4 on v2

--- a/solution.py
+++ b/solution.py
@@ -12,6 +12,7 @@
 CHUNKS = ((0, 1, 0), (1, 2, 1), (3, 2, 2), (5, 2, 3), (7, 1, 4))
 BOTH = tuple((half, way) for way in (0, 1) for half in (0, 1))
 STEP = (1, -1)
+FAR_FIRST = (4, 3, 5, 2, 6, 1, 7)
 HOP = {1: 1, 2: 2, 3: 1, 4: 2}
 
 
@@ -319,7 +320,7 @@
     send(sums_copy(0, 0))
     sums_copy(0, 0).wait_recv()
     sums_half[...] = sums[:, core] + sums_core[...]
-    for k in range(1, 8):
+    for k in FAR_FIRST:
         send(sums_copy(1, k))
     dense(0, 7)
     dense(1, 7)
@@ -334,10 +335,10 @@
         sums_copy(1, k).wait_recv()
         total = total + sums_y[k]
     sums_all[y, core] = total
-    for k in range(1, 8):
+    for k in FAR_FIRST:
         send(sums_copy(2, k))
     send(sums_copy(3, 0))
-    for k in range(1, 8):
+    for k in FAR_FIRST[::-1]:
         sums_copy(2, k).wait_recv()
         send(sums_copy(3, k))
     for k in range(8):

time: 78.7 us -> 77.6 us (0.986)
  the two profiles are of different devices: /device:TPU:5 before, /device:TPU:1 now
where the time goes in v4:
time: 77.6 us; the launch traced here: 77.5 us
  Pallas kernels  76.2 us (98%)
  between operations  1.29 us (2%)
    pallas_call x1, Pallas kernels, on_device(): pl.pallas_call(kernel, out_shape=(jax.ShapeDtypeStruct((448, 256), BF16),...  74.1 us
    pallas_call x1, Pallas kernels, on_device(): pl.pallas_call(finish, out_shape=(jax.ShapeDtypeStruct((448, 256), BF16),...  2.03 us

profile of v4, /device:TPU:1, one launch (start us, length us, event | category | flops | bytes accessed | tf_op | source)
XLA Modules:
  0.0 77.5 jit_solution(7365020124528032361)
XLA Ops:
  1.3 74.1 %shard_map.120 = (bf16[448,256]{1,0:T(8,128)(2,1)}, f32[8,2,40,128]{3,2,1,0:T(8,128)}) custom-call(bf16[256,128]{1,0:T(8,128)(2,1)} %gy_hbm.1, bf16[7,64,256]{2,1,0:T(8,128)(2,1)} %bitcast.6, bf16[448,8192]{1,0:T(8,128)(2,1)} %w_hbm.1, f32[16,448]{1,0:T(8,128)} %bitcast.8, f32[16,128]{1,0:T(8,128)} %b_hbm.1, f32[16,64,64]{2,1,0:T(8,128)} %vals_hbm.1, ...), custom_call_target="tpu_custom_call" | custom-call | flops 3000000000 | bytes 12000000 | tf_op jit(solution)/shard_map/pallas_call | solution.py:381
  75.4 2.0 %shard_map.121 = (bf16[448,256]{1,0:T(8,128)(2,1)}, f32[16,448]{1,0:T(8,128)}, f32[16,128]{1,0:T(8,128)}, f32[16,64,64]{2,1,0:T(8,128)}) custom-call(bf16[448,256]{1,0:T(8,128)(2,1)} %get-tuple-element.10.gh_in, f32[8,2,40,128]{3,2,1,0:T(8,128)} %get-tuple-element.11.sums_in), custom_call_target="tpu_custom_call" | custom-call | tf_op jit(solution)/shard_map/pallas_call | solution.py:431
